TPU v7x, 256 devices: a whole 4x4x8 slice. The times are simulated.
256 devices in a mesh: dp: 32 (over z, y_hi, core), ctx: 8 (over x, y_lo).
Axes of the slice: x: 4, y: 4 (y_hi: 2, y_lo: 2; y = y_hi * 2 + y_lo), z: 8, core: 2. Of those that a mesh axis runs over, the one named last changes fastest.
Arguments:
- q_heads: bfloat16 [32, 1536, 2048], P('dp', 'ctx'), may hold values from -8 to 8
- keys: bfloat16 [32, 1536, 128], P('dp', 'ctx'), may hold values from -8 to 8
- values: bfloat16 [32, 1536, 128], P('dp', 'ctx'), may hold values from -6 to 6
- out_grad: bfloat16 [32, 1536, 2048], P('dp', 'ctx'), may hold values from -0.29882812 to 0.29882812
- hidden_in: bfloat16 [32, 1536, 16384], P('dp', 'ctx'), may hold values from -6 to 6
- doc_lengths: int32 [32, 8], P('dp'), may hold values from 1 to 576, 1536 in all within a row
- span_order: int32 [16], replicated, may hold values from 0 to 15, each once
- m_codes: int32 [16384, 256], P('dp'), may hold values from -127 to 127
- m_scales: float32 [2048], P('dp'), may hold values from 0.05 to 0.5
- v_codes: int32 [16384, 256], P('dp'), may hold values from 1 to 255
- v_scales: float32 [2048], P('dp'), may hold values from 0.05 to 1
Outputs:
- dq: bfloat16 [32, 1536, 2048], P('dp', 'ctx')
- update: float32 [16384, 256], P('dp')
- m_norm: float32 [16384, 256], P('dp')
- m_absmax: float32 [2048], P('dp')
- v_norm: float32 [16384, 256], P('dp')
- v_absmax: float32 [2048], P('dp')
Inputs may be any that keep to these rules, and one draw needn't show every extreme that they name: `doc_lengths`: each sequence's 8 lengths sum to 1536. `span_order`: each stored block names a different position block.
All inputs are finite; a program needn't handle non-finite values. Where the computation divides by a largest or mean magnitude, that divisor is 1e-20 or more.
Results may differ from a plain program's by a relative error of at most 0.0078.
Values may be sent and summed in bfloat16 or wider, within the bound.
A program may use at most 128 MiB of HBM per device.

v0:
```python
import math
import jax
import jax.numpy as jnp
from jax import lax
from jax.sharding import PartitionSpec as P

BLOCK = 2048
STEP = 10


def positions(order, span, total):
    rows = jnp.arange(total, dtype=jnp.int32)
    slot = rows // span
    match = slot[:, None] == jnp.arange(order.shape[0], dtype=jnp.int32)[None, :]
    first = jnp.sum(jnp.where(match, order[None, :], 0), axis=1)
    return first * span + rows % span


def documents(pos, lengths):
    ends = jnp.cumsum(lengths)
    return jnp.sum((pos[:, None] >= ends[None, :]).astype(jnp.int32), axis=1)


def adam_blocks(grad, m_codes, m_scales, v_codes, v_scales):
    shape = grad.shape
    g_blocks = grad.reshape(-1, BLOCK)
    m_old = m_codes.reshape(-1, BLOCK).astype(jnp.float32) / 127.0 * m_scales[:, None]
    v_old = v_codes.reshape(-1, BLOCK).astype(jnp.float32) / 255.0 * v_scales[:, None]
    moment = 0.9 * m_old + 0.1 * g_blocks
    second = 0.95 * v_old + 0.05 * g_blocks * g_blocks
    update = moment / (1.0 - 0.9**STEP) / (jnp.sqrt(second / (1.0 - 0.95**STEP)) + 1e-08)
    m_absmax = jnp.max(jnp.abs(moment), axis=1)
    v_absmax = jnp.max(second, axis=1)
    m_norm = moment / (m_absmax[:, None] + 1e-06)
    v_norm = second / (v_absmax[:, None] + 1e-06)
    return (update.reshape(shape), m_norm.reshape(shape), m_absmax, v_norm.reshape(shape), v_absmax)


def contract_rows(left, right):
    return lax.dot_general(
        left, right, (((0,), (0,)), ((), ())), preferred_element_type=jnp.float32
    )


def contract_cols(left, right):
    return lax.dot_general(
        left, right, (((1,), (1,)), ((), ())), preferred_element_type=jnp.float32
    )


def shards(
    q_heads,
    keys,
    values,
    out_grad,
    hidden_in,
    doc_lengths,
    span_order,
    m_codes,
    m_scales,
    v_codes,
    v_scales,
):
    rows = q_heads.shape[1]
    head_dim = keys.shape[2]
    heads_width = q_heads.shape[2]
    nheads = heads_width // head_dim
    scale = 1.0 / math.sqrt(head_dim)
    total = rows * lax.axis_size("ctx")
    key_all, value_all = (
        lax.all_gather(keys[0], "ctx", axis=0, tiled=True),
        lax.all_gather(values[0], "ctx", axis=0, tiled=True),
    )
    pos = positions(span_order, rows // 2, total)
    doc = documents(pos, doc_lengths[0])
    first_row = lax.axis_index("ctx") * rows
    query_pos = lax.dynamic_slice_in_dim(pos, first_row, rows)
    query_doc = lax.dynamic_slice_in_dim(doc, first_row, rows)
    queries = q_heads[0].reshape(rows * nheads, head_dim)
    grads_out = out_grad[0].reshape(rows * nheads, head_dim)
    width = min(512, total)
    nblocks = total // width
    blocks = (
        key_all.reshape(nblocks, width, head_dim),
        value_all.reshape(nblocks, width, head_dim),
        pos.reshape(nblocks, width),
        doc.reshape(nblocks, width),
    )

    def block_masks(key_pos, key_doc):
        small = (key_pos[None, :] <= query_pos[:, None]) & (key_doc[None, :] == query_doc[:, None])
        wide = jnp.broadcast_to(small[:, None, :], (rows, nheads, width)).reshape(
            rows * nheads, width
        )
        return (small, wide)

    def forward_terms(carry, block):
        key_block, value_block, key_pos, key_doc = block
        small, wide = block_masks(key_pos, key_doc)
        top, denom, weighted = carry
        scores = contract_cols(queries, key_block) * scale
        dprob = contract_cols(grads_out, value_block)
        new_top = jnp.maximum(top, jnp.max(jnp.where(wide, scores, -1e30), axis=1, keepdims=True))
        expo = jnp.where(wide, jnp.exp(scores - new_top), 0.0)
        factor = jnp.exp(top - new_top)
        result = (
            new_top,
            denom * factor + jnp.sum(expo, axis=1, keepdims=True),
            weighted * factor + jnp.sum(expo * dprob, axis=1, keepdims=True),
        )
        return (result, None)

    column = jnp.zeros((rows * nheads, 1), jnp.float32)
    start_state = (column - 1e30, column, column)
    (top, denom, weighted), unused = lax.scan(forward_terms, start_state, blocks)
    delta = weighted / denom

    def backward_terms(accum, block):
        key_block, value_block, key_pos, key_doc = block
        small, wide = block_masks(key_pos, key_doc)
        acc = accum
        scores = contract_cols(queries, key_block) * scale
        dprob = contract_cols(grads_out, value_block)
        prob = jnp.where(wide, jnp.exp(scores - top), 0.0) / denom
        prob_low = prob.astype(jnp.bfloat16)
        dscore = (prob * (dprob - delta)).astype(jnp.bfloat16)
        acc = acc + jnp.dot(dscore, key_block, preferred_element_type=jnp.float32)
        dkey = contract_rows(dscore, queries) * scale
        dvalue = contract_rows(prob_low, grads_out)
        return (acc, jnp.concatenate([dkey, dvalue], axis=1))

    dq_sum, pieces = lax.scan(
        backward_terms, jnp.zeros((rows * nheads, head_dim), jnp.float32), blocks
    )
    dq = (dq_sum * scale).reshape(1, rows, heads_width).astype(jnp.bfloat16)
    partial_grads = pieces.reshape(total, 2 * head_dim)
    own = lax.psum_scatter(partial_grads, "ctx", scatter_dimension=0, tiled=True)
    own_low = own.astype(jnp.bfloat16)
    layer_in = hidden_in[0]
    grad = lax.psum_scatter(contract_rows(layer_in, own_low), "dp", scatter_dimension=0, tiled=True)
    grad = lax.psum(grad, "ctx")
    update, m_norm, m_absmax, v_norm, v_absmax = adam_blocks(
        grad, m_codes, m_scales, v_codes, v_scales
    )
    return (dq, update, m_norm, m_absmax, v_norm, v_absmax)


def solution(mesh):
    in_specs = (
        P("dp", "ctx", None),
        P("dp", "ctx", None),
        P("dp", "ctx", None),
        P("dp", "ctx", None),
        P("dp", "ctx", None),
        P("dp", None),
        P(),
        P("dp", None),
        P("dp"),
        P("dp", None),
        P("dp"),
    )
    out_specs = (
        P("dp", "ctx", None),
        P("dp", None),
        P("dp", None),
        P("dp"),
        P("dp", None),
        P("dp"),
    )
    return jax.shard_map(shards, mesh=mesh, in_specs=in_specs, out_specs=out_specs, check_vma=False)
```

profile of v0, /device:TPU:32, one launch (start us, length us, event | category | flops | bytes accessed | tf_op | source)
XLA Modules:
  0.0 549.1 jit_solution(15692817767166467675)
XLA Ops:
  11.0 29.1 %all-gather = bf16[1,1536,128]{2,1,0:T(8,128)(2,1)S(1)} all-gather(bf16[1,192,128]{2,1,0:T(8,128)(2,1)} %param.16), channel_id=2, replica_groups=mesh['dp'=32,'ctx'=8] {'ctx'}, dimensions={1}, use_global_device_ids=true | all-gather | bytes 442368 | tf_op jit(solution)/shard_map/all_gather | solution.py:71
  41.5 30.8 %all-gather.1 = bf16[1,1536,128]{2,1,0:T(8,128)(2,1)} all-gather(bf16[1,192,128]{2,1,0:T(8,128)(2,1)} %param.17), channel_id=3, replica_groups=mesh['dp'=32,'ctx'=8] {'ctx'}, dimensions={1}, use_global_device_ids=true | all-gather | bytes 442368 | tf_op jit(solution)/shard_map/all_gather | solution.py:72
  72.7 46.8 %while.28 = (s32[]{:T(128)}, f32[3072,1]{0,1:T(1,128)}, f32[3072,1]{0,1:T(1,128)}, f32[3072,1]{0,1:T(1,128)}, s32[3,512]{1,0:T(4,128)}, /*index=5*/s32[192]{0:T(...) while((s32[]{:T(128)}, f32[3072,1]{0,1:T(1,128)}, ...), condition=%wide.region_7.8_spmd.clone, body=%wide.region_3.7_spmd.clone.sunk | while | flops 824497152 | bytes 55990092 | solution.py:115
  74.7 1.7 copy.45
  76.4 3.9 fusion.79
  80.3 5.2 fusion.81
  89.8 1.7 copy.45
  91.5 3.9 fusion.79
  96.1 5.2 fusion.81
  107.3 3.8 fusion.79
  111.9 5.2 fusion.81
  120.9 55.8 %while.29 = (s32[]{:T(128)}, f32[3072,128]{1,0:T(8,128)}, f32[3,512,256]{2,1,0:T(8,128)}, s32[3,512]{1,0:T(4,128)}, s32[192]{0:T(256)S(1)}, /*index=5*/s32[3,512...) while((s32[]{:T(128)}, f32[3072,128]{1,0:T(8,128)}, ...), condition=%wide.region_9.10_spmd.clone, body=%wide.region_8.9_spmd.clone.sunk | while | flops 2027126784 | bytes 108267456 | solution.py:132
  123.0 1.7 copy.46
  124.7 1.9 fusion.94
  126.7 2.9 fusion.95
  129.7 2.2 convolution_add_fusion.2
  133.0 2.3 fusion.96
  135.3 2.3 convolution_multiply_fusion.2
  143.0 1.9 fusion.94
  145.0 2.9 fusion.95
  148.0 3.8 convolution_add_fusion.2
  151.7 2.3 fusion.96
  154.1 2.3 convolution_multiply_fusion.2
  161.8 1.9 fusion.94
  163.7 2.9 fusion.95
  166.7 3.8 convolution_add_fusion.2
  170.5 2.3 fusion.96
  172.8 2.3 convolution_multiply_fusion.2
  176.7 49.4 %reduce-scatter.3.cloned.1.call-done = f32[192,256]{1,0:T(8,128)} async-done(((f32[1536,256]{1,0:T(8,128)}), f32[192,256]{1,0:T(8,128)}) %reduce-scatter.3.cloned.1.call-update) | async-done | bytes 196624 | tf_op jit(solution)/shard_map/reduce_scatter | solution.py:137
  226.2 11.0 %convolution_bitcast_fusion = f32[16384,256]{0,1:T(8,128)} fusion(bf16[1,192,16384]{2,1,0:T(8,128)(2,1)} %param.19, f32[192,256]{1,0:T(8,128)} %reduce-scatter.3.cloned.1.call-done), kind=kOutput, calls=%fused_computation.49 | convolution fusion | flops 1610661888 | bytes 23265280 | tf_op jit(solution)/shard_map/dot_general | solution.py:40
  237.3 218.4 %reduce-scatter.5.cloned.1.call-done = f32[512,256]{0,1:T(8,128)} async-done(((f32[16384,256]{0,1:T(8,128)}), f32[512,256]{0,1:T(8,128)}) %reduce-scatter.5.cloned.1.call-update) | async-done | bytes 524304 | tf_op jit(solution)/shard_map/reduce_scatter | solution.py:140
  457.9 79.3 %all-reduce.2.cloned.1.call-done = f32[512,256]{0,1:T(8,128)} async-done(((f32[512,256]{0,1:T(8,128)}), f32[512,256]{0,1:T(8,128)}) %all-reduce.2.cloned.1.call-update) | async-done | bytes 524304 | tf_op jit(solution)/shard_map/psum | solution.py:141
  (197 shorter events, 45.8 us)
Async XLA Ops:
  7.2 65.2 %copy-start.10 = (bf16[1,192,2048]{2,1,0:T(8,128)(2,1)S(1)}, bf16[1,192,2048]{2,1,0:T(8,128)(2,1)}, u32[]{:S(2)}) copy-start(bf16[1,192,2048]{2,1,0:T(8,128)(2,1)} %param.18) | copy-start | bytes 2359300
  7.2 219.0 %reduce-scatter.3.cloned.1.call-start = ((), (), s32[]{:S(2)}) async-start(), calls=%async_computation.2 | async-start | bytes 1769472 | tf_op jit(solution)/shard_map/reduce_scatter | solution.py:137
  80.3 5.2 copy-start
  96.1 5.2 copy-start
  111.9 5.2 copy-start
  120.9 5.8 %copy-start.4 = (bf16[3072,128]{1,0:T(8,128)(2,1)}, bf16[3072,128]{1,0:T(8,128)(2,1)S(1)}, u32[]{:S(2)}) copy-start(bf16[3072,128]{1,0:T(8,128)(2,1)S(1)} %get-tuple-element.577) | copy-start | bytes 2359300 | tf_op jit(solution)/shard_map/while
  120.9 5.8 %copy-start.6 = (bf16[3072,128]{1,0:T(8,128)(2,1)}, bf16[3072,128]{1,0:T(8,128)(2,1)S(1)}, u32[]{:S(2)}) copy-start(bf16[3072,128]{1,0:T(8,128)(2,1)S(1)} %get-tuple-element.581) | copy-start | bytes 2359300 | tf_op jit(solution)/shard_map/while
  120.9 3.8 copy-start.9
  120.9 3.8 copy-start.16
  126.7 3.0 copy-start.1
  129.7 3.4 copy-start.2
  139.2 5.8 %copy-start.4 = (bf16[3072,128]{1,0:T(8,128)(2,1)}, bf16[3072,128]{1,0:T(8,128)(2,1)S(1)}, u32[]{:S(2)}) copy-start(bf16[3072,128]{1,0:T(8,128)(2,1)S(1)} %get-tuple-element.577) | copy-start | bytes 2359300 | tf_op jit(solution)/shard_map/while
  139.2 5.8 %copy-start.6 = (bf16[3072,128]{1,0:T(8,128)(2,1)}, bf16[3072,128]{1,0:T(8,128)(2,1)S(1)}, u32[]{:S(2)}) copy-start(bf16[3072,128]{1,0:T(8,128)(2,1)S(1)} %get-tuple-element.581) | copy-start | bytes 2359300 | tf_op jit(solution)/shard_map/while
  139.2 3.8 copy-start.9
  139.2 3.8 copy-start.16
  145.0 3.0 copy-start.1
  148.0 3.8 copy-start.2
  157.9 5.8 %copy-start.4 = (bf16[3072,128]{1,0:T(8,128)(2,1)}, bf16[3072,128]{1,0:T(8,128)(2,1)S(1)}, u32[]{:S(2)}) copy-start(bf16[3072,128]{1,0:T(8,128)(2,1)S(1)} %get-tuple-element.577) | copy-start | bytes 2359300 | tf_op jit(solution)/shard_map/while
  157.9 5.8 %copy-start.6 = (bf16[3072,128]{1,0:T(8,128)(2,1)}, bf16[3072,128]{1,0:T(8,128)(2,1)S(1)}, u32[]{:S(2)}) copy-start(bf16[3072,128]{1,0:T(8,128)(2,1)S(1)} %get-tuple-element.581) | copy-start | bytes 2359300 | tf_op jit(solution)/shard_map/while
  157.9 3.8 copy-start.9
  157.9 3.8 copy-start.16
  163.7 3.0 copy-start.1
  166.7 3.8 copy-start.2
  176.7 279.0 %reduce-scatter.5.cloned.1.call-start = ((), (), s32[]{:S(2)}) async-start(), calls=%async_computation.3 | async-start | bytes 17301504 | tf_op jit(solution)/shard_map/reduce_scatter | solution.py:140
  237.2 218.6 %copy-start.3 = (f32[3072,128]{1,0:T(8,128)S(1)}, f32[3072,128]{1,0:T(8,128)}, u32[]{:S(2)}) copy-start(f32[3072,128]{1,0:T(8,128)} %get-tuple-element.146) | copy-start | bytes 4718596
  237.2 219.9 %copy-start.21 = (f32[64]{0:T(128)S(1)}, f32[64]{0:T(128)}, u32[]{:S(2)}) copy-start(f32[64]{0:T(128)} %param.23) | copy-start | bytes 772
  237.2 220.1 %copy-start.11 = (s32[512,256]{1,0:T(8,128)S(1)}, s32[512,256]{1,0:T(8,128)}, u32[]{:S(2)}) copy-start(s32[512,256]{1,0:T(8,128)} %param.22) | copy-start | bytes 1572868
  237.2 220.3 %copy-start.22 = (f32[64]{0:T(128)S(1)}, f32[64]{0:T(128)}, u32[]{:S(2)}) copy-start(f32[64]{0:T(128)} %param.25) | copy-start | bytes 772
  237.2 220.4 %copy-start.12 = (s32[512,256]{1,0:T(8,128)S(1)}, s32[512,256]{1,0:T(8,128)}, u32[]{:S(2)}) copy-start(s32[512,256]{1,0:T(8,128)} %param.24) | copy-start | bytes 1572868
  237.2 300.0 %all-reduce.2.cloned.1.call-start = ((), (), s32[]{:S(2)}) async-start(), calls=%async_computation.4 | async-start | bytes 1048576 | tf_op jit(solution)/shard_map/psum | solution.py:141
  538.7 3.9 copy-start.19
  539.1 3.5 copy-start.20
  (24 other events, 33.0 us)
Sparse Core Ops, SparseCore 0:
  176.8 49.3 reduce-scatter.2
  237.3 218.3 reduce-scatter.4
  458.5 78.6 all-reduce.1
where the time goes:
time: 550 us; the launch traced here: 549 us
  waiting for transfers between devices  347 us (63%)
  matrix products  76.2 us (14%)
  blocking collectives  59.9 us (11%)
  local copies, waits for them, and re-layouts  33.6 us (6%)
  other arithmetic  17.2 us (3%)
  between operations  14 us (3%)
    reduce_scatter x1, waiting for transfers between devices, shards(): lax.psum_scatter(contract_rows(layer_in, own_low), 'dp', scatter_dimensio...  218 us
    psum x1, waiting for transfers between devices, shards(): grad = lax.psum(grad, 'ctx')  79.3 us
    reduce_scatter x1, waiting for transfers between devices, shards(): lax.psum_scatter(partial_grads, 'ctx', scatter_dimension=0, tiled=True)  49.4 us
    dot_general x12, matrix products, contract_cols(): lax.dot_general(left, right, (((1,), (1,)), ((), ())), preferred_element_...  41.6 us
    all_gather x1, blocking collectives, shards(): lax.all_gather(values[0], 'ctx', axis=0, tiled=True)  30.8 us
    all_gather x1, blocking collectives, shards(): lax.all_gather(keys[0], 'ctx', axis=0, tiled=True)  29.1 us
    dot_general x7, matrix products, contract_rows(): lax.dot_general(left, right, (((0,), (0,)), ((), ())), preferred_element_...  24.8 us
  transfers between devices with their start and end apart: 3, of which 3 were waited for; matrix products, arithmetic and copies ran while one was open for 0% of the time, Pallas kernels for 0%

commit v1 on v0

--- a/solution.py
+++ b/solution.py
@@ -69,7 +69,9 @@
     total = rows * lax.axis_size("ctx")
     key_all, value_all = (
         lax.all_gather(keys[0], "ctx", axis=0, tiled=True),
-        lax.all_gather(values[0], "ctx", axis=0, tiled=True),
+        jnp.concatenate(
+            lax.all_to_all(jnp.stack([values[0]] * lax.axis_size("ctx")), "ctx", 0, 0), axis=0
+        ),
     )
     pos = positions(span_order, rows // 2, total)
     doc = documents(pos, doc_lengths[0])

time: 550 us -> 526 us (0.956)
  blocking collectives: 59.9 us -> 29.2 us
    all_gather x1 -> x0, blocking collectives: 30.8 us -> none  [shards(): lax.all_gather(values[0], 'ctx', axis=0, tiled=True)]
  transfers between devices with their start and end apart: 3 -> 4, of which waited for: 3 -> 3; matrix products, arithmetic and copies ran while one was open for 0% -> 2% of each run, Pallas kernels for 0% -> 0%
where the time goes in v1:
time: 526 us; the launch traced here: 525 us
  waiting for transfers between devices  345 us (66%)
  matrix products  75.8 us (14%)
  local copies, waits for them, and re-layouts  37 us (7%)
  blocking collectives  29.2 us (6%)
  other arithmetic  16.9 us (3%)
  between operations  14 us (3%)
  starting transfers between devices  5.43 us (1%)
    reduce_scatter x1, waiting for transfers between devices, shards(): lax.psum_scatter(contract_rows(layer_in, own_low), 'dp', scatter_dimensio...  216 us
    psum x1, waiting for transfers between devices, shards(): grad = lax.psum(grad, 'ctx')  80.1 us
    reduce_scatter x1, waiting for transfers between devices, shards(): lax.psum_scatter(partial_grads, 'ctx', scatter_dimension=0, tiled=True)  49.2 us
    dot_general x12, matrix products, contract_cols(): lax.dot_general(left, right, (((1,), (1,)), ((), ())), preferred_element_...  41.2 us
    all_gather x1, blocking collectives, shards(): lax.all_gather(keys[0], 'ctx', axis=0, tiled=True)  29.2 us
    dot_general x7, matrix products, contract_rows(): lax.dot_general(left, right, (((0,), (0,)), ((), ())), preferred_element_...  24.8 us
  transfers between devices with their start and end apart: 4, of which 3 were waited for; matrix products, arithmetic and copies ran while one was open for 2% of the time, Pallas kernels for 0%

profile of v1, /device:TPU:32, one launch (start us, length us, event | category | flops | bytes accessed | tf_op | source)
XLA Modules:
  0.0 524.6 jit_solution(7572806509579815984)
XLA Ops:
  8.9 5.3 %all-to-all-start = ((bf16[8,192,128]{2,1,0:T(8,128)(2,1)}), bf16[8,192,128]{2,1,0:T(8,128)(2,1)}, u32[]{:S(2)}, u32[]{:S(2)}) async-start(bf16[8,192,128]{2,1,0:T(8,128)(2,1)} %stack.3), calls=%async_computation | async-start | bytes 786432 | tf_op jit(solution)/shard_map/all_to_all | solution.py:73
  19.1 29.2 %all-gather = bf16[1,1536,128]{2,1,0:T(8,128)(2,1)S(1)} all-gather(bf16[1,192,128]{2,1,0:T(8,128)(2,1)S(1)} %copy-done.17), channel_id=2, replica_groups=mesh['dp'=32,'ctx'=8] {'ctx'}, dimensions={1}, use_global_device_ids=true | all-gather | bytes 442368 | tf_op jit(solution)/shard_map/all_gather | solution.py:71
  48.9 46.7 %while.28 = (s32[]{:T(128)}, f32[3072,1]{0,1:T(1,128)}, f32[3072,1]{0,1:T(1,128)}, f32[3072,1]{0,1:T(1,128)}, s32[3,512]{1,0:T(4,128)}, /*index=5*/s32[192]{0:T(...) while((s32[]{:T(128)}, f32[3072,1]{0,1:T(1,128)}, ...), condition=%wide.region_7.8_spmd.clone, body=%wide.region_3.7_spmd.clone.sunk | while | flops 824497152 | bytes 55990092 | solution.py:117
  50.8 1.7 copy.45
  52.5 3.8 fusion.79
  56.4 5.2 fusion.81
  65.9 1.7 copy.45
  67.6 3.8 fusion.79
  72.2 5.2 fusion.81
  83.4 3.8 fusion.79
  88.0 5.2 fusion.81
  96.9 55.2 %while.29 = (s32[]{:T(128)}, f32[3072,128]{1,0:T(8,128)}, f32[3,512,256]{2,1,0:T(8,128)}, s32[3,512]{1,0:T(4,128)}, s32[192]{0:T(256)S(1)}, /*index=5*/s32[3,512...) while((s32[]{:T(128)}, f32[3072,128]{1,0:T(8,128)}, ...), condition=%wide.region_9.10_spmd.clone, body=%wide.region_8.9_spmd.clone.sunk | while | flops 2027126784 | bytes 108218272 | solution.py:134
  99.0 1.7 copy.46
  100.7 1.9 fusion.94
  102.7 2.8 fusion.95
  105.5 2.2 convolution_add_fusion.2
  108.9 2.3 fusion.96
  111.2 2.3 convolution_multiply_fusion.2
  118.8 1.9 fusion.94
  120.8 2.8 fusion.95
  123.6 3.8 convolution_add_fusion.2
  127.4 2.3 fusion.96
  129.7 2.3 convolution_multiply_fusion.2
  137.4 1.9 fusion.94
  139.4 2.8 fusion.95
  142.2 3.8 convolution_add_fusion.2
  146.0 2.3 fusion.96
  148.3 2.3 convolution_multiply_fusion.2
  152.2 49.2 %reduce-scatter.3.cloned.1.call-done = f32[192,256]{1,0:T(8,128)} async-done(((f32[1536,256]{1,0:T(8,128)}), f32[192,256]{1,0:T(8,128)}) %reduce-scatter.3.cloned.1.call-update) | async-done | bytes 196624 | tf_op jit(solution)/shard_map/reduce_scatter | solution.py:139
  201.4 11.0 %convolution_bitcast_fusion = f32[16384,256]{0,1:T(8,128)} fusion(bf16[1,192,16384]{2,1,0:T(8,128)(2,1)} %param.19, f32[192,256]{1,0:T(8,128)} %reduce-scatter.3.cloned.1.call-done), kind=kOutput, calls=%fused_computation.49 | convolution fusion | flops 1610661888 | bytes 23265280 | tf_op jit(solution)/shard_map/dot_general | solution.py:40
  215.1 216.1 %reduce-scatter.5.cloned.1.call-done = f32[512,256]{0,1:T(8,128)} async-done(((f32[16384,256]{0,1:T(8,128)}), f32[512,256]{0,1:T(8,128)}) %reduce-scatter.5.cloned.1.call-update) | async-done | bytes 524304 | tf_op jit(solution)/shard_map/reduce_scatter | solution.py:142
  432.6 80.1 %all-reduce.2.cloned.1.call-done = f32[512,256]{0,1:T(8,128)} async-done(((f32[512,256]{0,1:T(8,128)}), f32[512,256]{0,1:T(8,128)}) %all-reduce.2.cloned.1.call-update) | async-done | bytes 524304 | tf_op jit(solution)/shard_map/psum | solution.py:143
  (193 shorter events, 49.0 us)
Async XLA Ops:
  7.2 11.5 %copy-start.10 = (bf16[1,192,2048]{2,1,0:T(8,128)(2,1)S(1)}, bf16[1,192,2048]{2,1,0:T(8,128)(2,1)}, u32[]{:S(2)}) copy-start(bf16[1,192,2048]{2,1,0:T(8,128)(2,1)} %param.18) | copy-start | bytes 2359300
  7.2 11.9 %copy-start.17 = (bf16[1,192,128]{2,1,0:T(8,128)(2,1)S(1)}, bf16[1,192,128]{2,1,0:T(8,128)(2,1)}, u32[]{:S(2)}) copy-start(bf16[1,192,128]{2,1,0:T(8,128)(2,1)} %param.16) | copy-start | bytes 147460
  8.9 40.0 %all-to-all-start = ((bf16[8,192,128]{2,1,0:T(8,128)(2,1)}), bf16[8,192,128]{2,1,0:T(8,128)(2,1)}, u32[]{:S(2)}, u32[]{:S(2)}) async-start(bf16[8,192,128]{2,1,0:T(8,128)(2,1)} %stack.3), calls=%async_computation | async-start | bytes 786432 | tf_op jit(solution)/shard_map/all_to_all | solution.py:73
  14.2 187.2 %reduce-scatter.3.cloned.1.call-start = ((), (), s32[]{:S(2)}) async-start(), calls=%async_computation.3 | async-start | bytes 1769472 | tf_op jit(solution)/shard_map/reduce_scatter | solution.py:139
  56.4 5.2 copy-start
  61.6 1.7 copy-start.8
  72.2 5.2 copy-start
  77.4 1.7 copy-start.8
  88.0 5.2 copy-start
  96.9 5.7 %copy-start.4 = (bf16[3072,128]{1,0:T(8,128)(2,1)}, bf16[3072,128]{1,0:T(8,128)(2,1)S(1)}, u32[]{:S(2)}) copy-start(bf16[3072,128]{1,0:T(8,128)(2,1)S(1)} %get-tuple-element.577) | copy-start | bytes 2359300 | tf_op jit(solution)/shard_map/while
  96.9 5.7 %copy-start.6 = (bf16[3072,128]{1,0:T(8,128)(2,1)}, bf16[3072,128]{1,0:T(8,128)(2,1)S(1)}, u32[]{:S(2)}) copy-start(bf16[3072,128]{1,0:T(8,128)(2,1)S(1)} %get-tuple-element.581) | copy-start | bytes 2359300 | tf_op jit(solution)/shard_map/while
  96.9 3.8 copy-start.9
  96.9 3.8 copy-start.14
  102.7 2.8 copy-start.1
  105.5 3.4 copy-start.2
  115.0 5.7 %copy-start.4 = (bf16[3072,128]{1,0:T(8,128)(2,1)}, bf16[3072,128]{1,0:T(8,128)(2,1)S(1)}, u32[]{:S(2)}) copy-start(bf16[3072,128]{1,0:T(8,128)(2,1)S(1)} %get-tuple-element.577) | copy-start | bytes 2359300 | tf_op jit(solution)/shard_map/while
  115.0 5.7 %copy-start.6 = (bf16[3072,128]{1,0:T(8,128)(2,1)}, bf16[3072,128]{1,0:T(8,128)(2,1)S(1)}, u32[]{:S(2)}) copy-start(bf16[3072,128]{1,0:T(8,128)(2,1)S(1)} %get-tuple-element.581) | copy-start | bytes 2359300 | tf_op jit(solution)/shard_map/while
  115.0 3.8 copy-start.9
  115.0 3.8 copy-start.14
  120.8 2.8 copy-start.1
  123.6 3.8 copy-start.2
  133.6 5.7 %copy-start.4 = (bf16[3072,128]{1,0:T(8,128)(2,1)}, bf16[3072,128]{1,0:T(8,128)(2,1)S(1)}, u32[]{:S(2)}) copy-start(bf16[3072,128]{1,0:T(8,128)(2,1)S(1)} %get-tuple-element.577) | copy-start | bytes 2359300 | tf_op jit(solution)/shard_map/while
  133.6 5.7 %copy-start.6 = (bf16[3072,128]{1,0:T(8,128)(2,1)}, bf16[3072,128]{1,0:T(8,128)(2,1)S(1)}, u32[]{:S(2)}) copy-start(bf16[3072,128]{1,0:T(8,128)(2,1)S(1)} %get-tuple-element.581) | copy-start | bytes 2359300 | tf_op jit(solution)/shard_map/while
  133.6 3.8 copy-start.9
  133.6 3.8 copy-start.14
  139.3 2.8 copy-start.1
  142.2 3.8 copy-start.2
  152.2 279.0 %reduce-scatter.5.cloned.1.call-start = ((), (), s32[]{:S(2)}) async-start(), calls=%async_computation.4 | async-start | bytes 17301504 | tf_op jit(solution)/shard_map/reduce_scatter | solution.py:142
  212.4 218.8 %copy-start.3 = (f32[3072,128]{1,0:T(8,128)S(1)}, f32[3072,128]{1,0:T(8,128)}, u32[]{:S(2)}) copy-start(f32[3072,128]{1,0:T(8,128)} %get-tuple-element.146) | copy-start | bytes 4718596
  212.5 300.3 %all-reduce.2.cloned.1.call-start = ((), (), s32[]{:S(2)}) async-start(), calls=%async_computation.5 | async-start | bytes 1048576 | tf_op jit(solution)/shard_map/psum | solution.py:143
  514.2 3.9 copy-start.18
  514.6 3.5 copy-start.19
  (22 other events, 26.6 us)
Sparse Core Ops, SparseCore 0:
  152.3 49.0 reduce-scatter.2
  212.6 218.5 reduce-scatter.4
  434.0 78.6 all-reduce.1
